TPU v7x, 32 devices: a whole 2x2x4 slice. The times are simulated.
32 devices in a mesh: groups: 2 (over y), tok: 4 (over z), blk: 2 (over x), sub: 2 (over core).
Axes of the slice: x: 2, y: 2, z: 4, core: 2. Of those that a mesh axis runs over, the one named last changes fastest.
Arguments:
- features_in: bfloat16 [256, 4096], P(('groups', 'tok'), 'blk'), parts along dimension 0, may hold values from -6 to 6
- gate_tiles: bfloat16 [128, 2, 12, 128, 128], P(('tok', 'sub'), 'blk'), may hold values from -0.125 to 0.125
- up_tiles: bfloat16 [128, 2, 12, 128, 128], P(('tok', 'sub'), 'blk'), may hold values from -0.125 to 0.125
- block_rows: int32 [128, 2, 12], P(('tok', 'sub'), 'blk'), may hold values from 0 to 15, as said below
- block_counts: int32 [128, 2], P(('tok', 'sub'), 'blk'), may hold values from 4 to 12
- d_hidden: bfloat16 [256, 16384], P(('groups', 'blk'), ('tok', 'sub')), parts along dimension 0, may hold values from -6 to 6
Outputs:
- hidden: bfloat16 [256, 16384], P(('groups', 'blk'), ('tok', 'sub')), parts along dimension 0
- gate_tiles_grad: bfloat16 [256, 2, 12, 128, 128], P(('groups', 'tok', 'sub'), 'blk'), parts along dimension 0
- up_tiles_grad: bfloat16 [256, 2, 12, 128, 128], P(('groups', 'tok', 'sub'), 'blk'), parts along dimension 0
- features_grad: bfloat16 [256, 4096], P(('groups', 'tok'), 'blk'), parts along dimension 0
There are 2 independent parts, one for each index of `groups`. A program takes and returns all parts, laid end to end along the dimension named above; an argument that names none is the same for every part. Nothing has to cross between parts.
Inputs may be any that keep to these rules, and one draw needn't show every extreme that they name: `block_rows`: the 12 entries of one list are distinct local row-block indices; only the first block_counts of them are kept.
All inputs are finite; a program needn't handle non-finite values.
Results may differ from a plain program's by a relative error of at most 0.015.
Values may be sent and summed in bfloat16 or wider, within the bound.
No kernel may reach another device: no remote copies, remote signals or barrier semaphores. Data moves between devices by JAX's collectives and lax.ppermute only.
A program may use at most 128 MiB of HBM per device.

v0:
```python
import functools

import jax
import jax.numpy as jnp
from jax import lax
from jax.experimental import pallas as pl
from jax.experimental.pallas import tpu as pltpu
from jax.sharding import PartitionSpec as P

F32 = jnp.float32
BF16 = jnp.bfloat16
MIB = 1 << 20
VMEM_SPEC = pl.BlockSpec(memory_space=pltpu.VMEM)
SMEM_SPEC = pl.BlockSpec(memory_space=pltpu.SMEM)
ANY_SPEC = pl.BlockSpec(memory_space=pl.ANY)


def limit(mib):
    return pltpu.CompilerParams(vmem_limit_bytes=mib * MIB)


def lanes(index, width):
    return pl.ds(pl.multiple_of(index * width, width), width)


def weights_of(c, gate_ref, up_ref):
    slots, rows, cols = gate_ref.shape[2:]
    return jnp.concatenate(
        [gate_ref[c, 0].reshape(slots * rows, cols), up_ref[c, 0].reshape(slots * rows, cols)], axis=1
    )


def forward_column(c, rows_ref, counts_ref, x_ref, gate_ref, up_ref, part_ref):
    slots, tile = gate_ref.shape[2:4]
    count = counts_ref[c, 0]
    picked = []
    for k in range(slots):
        block = x_ref[:, lanes(rows_ref[c, 0, k], tile)]
        picked.append(jnp.where(k < count, block, jnp.zeros_like(block)))
    part_ref[c] = jnp.dot(
        jnp.concatenate(picked, axis=1), weights_of(c, gate_ref, up_ref), preferred_element_type=F32
    ).astype(BF16)


def load_forward_kernel(rows_ref, counts_ref, x_ref, gate_hbm, up_hbm, part_ref, gate_ref, up_ref, sems):
    cols = gate_ref.shape[0]

    def copies(c):
        return (
            pltpu.make_async_copy(gate_hbm.at[c], gate_ref.at[c], sems.at[0, c]),
            pltpu.make_async_copy(up_hbm.at[c], up_ref.at[c], sems.at[1, c]),
        )

    for c in range(cols):
        for copy in copies(c):
            copy.start()

    def body(c, carry):
        for copy in copies(c):
            copy.wait()
        forward_column(c, rows_ref, counts_ref, x_ref, gate_ref, up_ref, part_ref)
        return carry

    lax.fori_loop(0, cols, body, 0)


def forward_kernel(rows_ref, counts_ref, x_ref, gate_ref, up_ref, part_ref):
    def body(c, carry):
        forward_column(c, rows_ref, counts_ref, x_ref, gate_ref, up_ref, part_ref)
        return carry

    lax.fori_loop(0, gate_ref.shape[0], body, 0, unroll=2)


def backward_kernel(owners, step, meta_ref, rows_ref, counts_ref, gate_ref, up_ref, *refs):
    parts = refs[:owners]
    cots = refs[owners : 2 * owners]
    hidden_ref, grads_ref, dx_ref, cot_ref, acc_ref, sem = refs[2 * owners :]
    cols, _, slots, tile, _ = gate_ref.shape
    shard_rows = cot_ref.shape[0]
    shards_each = cots[0].shape[0] // shard_rows
    shard = meta_ref[0] ^ step
    source = (shard // shards_each) ^ meta_ref[1]
    first_row = pl.multiple_of((shard % shards_each) * shard_rows, shard_rows)
    for i, cot in enumerate(cots):

        @pl.when(source == i)
        def _(cot=cot):
            pltpu.make_async_copy(cot.at[pl.ds(first_row, shard_rows)], cot_ref, sem).start()

    acc_ref[...] = jnp.zeros_like(acc_ref)
    pltpu.make_async_copy(cots[0].at[pl.ds(0, shard_rows)], cot_ref, sem).wait()

    def body(c, carry):
        total = parts[0][c].astype(F32)
        for part in parts[1:]:
            total = total + part[c].astype(F32)
        gate_value, up_value = total[:, :tile], total[:, tile:]
        cotangent = cot_ref[:, lanes(c, tile)].astype(F32)
        sig_gate = jax.nn.sigmoid(gate_value)
        act_gate = gate_value * sig_gate
        hidden_ref[:, lanes(c, tile)] = (act_gate * up_value).astype(BF16)
        gate_grad = (cotangent * up_value * sig_gate * (1.0 + gate_value * (1.0 - sig_gate))).astype(BF16)
        up_grad = (cotangent * act_gate).astype(BF16)
        grads = jnp.concatenate([gate_grad, up_grad], axis=1)
        grads_ref[c] = grads
        back = lax.dot_general(
            grads, weights_of(c, gate_ref, up_ref), (((1,), (1,)), ((), ())), preferred_element_type=F32
        )
        count = counts_ref[c, 0]
        for k in range(slots):
            row = rows_ref[c, 0, k]
            term = back[:, k * tile : (k + 1) * tile]
            acc_ref[row] += jnp.where(k < count, term, jnp.zeros_like(term))
        return carry

    lax.fori_loop(0, cols, body, 0, unroll=2)
    for r in range(acc_ref.shape[0]):
        dx_ref[:, r * tile : (r + 1) * tile] = acc_ref[r].astype(BF16)


def tile_grads_kernel(shards, meta_ref, rows_ref, counts_ref, *refs):
    xs = refs[:shards]
    grads = refs[shards : 2 * shards]
    hiddens = refs[2 * shards : 3 * shards]
    gate_hbm, up_hbm, hidden_hbm, turned_ref, gate_ref, up_ref, sems, hidden_sems = refs[3 * shards :]
    cols, _, slots, tile, _ = gate_ref.shape
    shard_rows = hiddens[0].shape[0]
    shards_each = hidden_hbm.shape[0] // shard_rows

    def hidden_copy(i, source):
        return pltpu.make_async_copy(
            source, hidden_hbm.at[pl.ds(i * shard_rows, shard_rows)], hidden_sems.at[i]
        )

    for i in range(shards_each):
        step = (meta_ref[1] * shards_each + i) ^ meta_ref[0]
        for j in range(shards):

            @pl.when(step == j)
            def _(i=i, j=j):
                hidden_copy(i, hiddens[j]).start()

    for r in range(turned_ref.shape[0]):
        block = jnp.concatenate([x[:, r * tile : (r + 1) * tile] for x in xs], axis=0)
        turned_ref[r] = block.T

    def copies(c):
        return (
            pltpu.make_async_copy(gate_ref.at[c], gate_hbm.at[c], sems.at[0, c]),
            pltpu.make_async_copy(up_ref.at[c], up_hbm.at[c], sems.at[1, c]),
        )

    def body(c, carry):
        picked = jnp.concatenate([turned_ref[rows_ref[c, 0, k]] for k in range(slots)], axis=0)
        grad = jnp.concatenate([g[c] for g in grads], axis=0)
        found = jnp.dot(picked, grad, preferred_element_type=F32)
        count = counts_ref[c, 0]
        for k in range(slots):
            term = found[k * tile : (k + 1) * tile]
            term = jnp.where(k < count, term, jnp.zeros_like(term)).astype(BF16)
            gate_ref[c, 0, k] = term[:, :tile]
            up_ref[c, 0, k] = term[:, tile:]
        for copy in copies(c):
            copy.start()
        return carry

    lax.fori_loop(0, cols, body, 0)

    def finish(c, carry):
        for copy in copies(c):
            copy.wait()
        return carry

    lax.fori_loop(0, cols, finish, 0)
    for i in range(shards_each):
        hidden_copy(i, hiddens[0]).wait()


def swap(x, axis, step):
    return lax.ppermute(x, axis, [(i, i ^ step) for i in range(lax.axis_size(axis))])


def on_device(features_in, gate_tiles, up_tiles, block_rows, block_counts, d_hidden):
    shards, owners = lax.axis_size("tok"), lax.axis_size("blk")
    cols, _, slots, tile, _ = gate_tiles.shape
    shard_rows, width = features_in.shape
    row_blocks = width // tile
    hidden_cols = cols * tile
    meta = jnp.stack([lax.axis_index("tok"), lax.axis_index("blk")]).astype(jnp.int32)

    cots = [d_hidden] + [swap(d_hidden, "blk", s) for s in range(1, owners)]
    xs = [features_in] + [swap(features_in, "tok", s) for s in range(1, shards)]

    part_shape = jax.ShapeDtypeStruct((cols, shard_rows, 2 * tile), BF16)
    macs = shard_rows * cols * slots * tile * tile * 2
    weight_bytes = 2 * cols * slots * tile * tile * 2
    part, gate_held, up_held = pl.pallas_call(
        load_forward_kernel,
        out_shape=(
            part_shape,
            pltpu.VMEM(gate_tiles.shape, BF16),
            pltpu.VMEM(up_tiles.shape, BF16),
        ),
        in_specs=[SMEM_SPEC, SMEM_SPEC, VMEM_SPEC, ANY_SPEC, ANY_SPEC],
        out_specs=(VMEM_SPEC, VMEM_SPEC, VMEM_SPEC),
        scratch_shapes=[pltpu.SemaphoreType.DMA((2, cols))],
        compiler_params=limit(16),
        cost_estimate=pl.CostEstimate(flops=2 * macs, bytes_accessed=weight_bytes, transcendentals=0),
        name="load_forward",
    )(block_rows, block_counts, features_in, gate_tiles, up_tiles)
    parts = [part]
    for s in range(1, shards):
        parts.append(
            pl.pallas_call(
                forward_kernel,
                out_shape=part_shape,
                in_specs=[SMEM_SPEC, SMEM_SPEC, VMEM_SPEC, VMEM_SPEC, VMEM_SPEC],
                out_specs=VMEM_SPEC,
                compiler_params=limit(16),
                cost_estimate=pl.CostEstimate(flops=2 * macs, bytes_accessed=weight_bytes, transcendentals=0),
                name="forward",
            )(block_rows, block_counts, xs[s], gate_held, up_held)
        )
    others = [[swap(part, "blk", s) for s in range(1, owners)] for part in parts]

    hiddens, grads, dxs = [], [], []
    for s in range(shards):
        hidden, grad, dx = pl.pallas_call(
            functools.partial(backward_kernel, owners, s),
            out_shape=(
                jax.ShapeDtypeStruct((shard_rows, hidden_cols), BF16),
                part_shape,
                jax.ShapeDtypeStruct((shard_rows, width), BF16),
            ),
            in_specs=[SMEM_SPEC] * 3 + [VMEM_SPEC] * (2 + owners) + [ANY_SPEC] * owners,
            out_specs=(VMEM_SPEC, VMEM_SPEC, VMEM_SPEC),
            scratch_shapes=[
                pltpu.VMEM((shard_rows, hidden_cols), BF16),
                pltpu.VMEM((row_blocks, shard_rows, tile), F32),
                pltpu.SemaphoreType.DMA,
            ],
            compiler_params=limit(16),
            cost_estimate=pl.CostEstimate(flops=2 * macs, bytes_accessed=weight_bytes, transcendentals=0),
            name="backward",
        )(meta, block_rows, block_counts, gate_held, up_held, parts[s], *others[s], *cots)
        hiddens.append(hidden)
        grads.append(grad)
        dxs.append(dx)

    arrived = [dxs[0]] + [swap(dxs[s], "tok", s) for s in range(1, shards)]

    gate_out, up_out, hidden_out = pl.pallas_call(
        functools.partial(tile_grads_kernel, shards),
        out_shape=(
            jax.ShapeDtypeStruct(gate_tiles.shape, BF16),
            jax.ShapeDtypeStruct(up_tiles.shape, BF16),
            jax.ShapeDtypeStruct(d_hidden.shape, BF16),
        ),
        in_specs=[SMEM_SPEC] * 3 + [VMEM_SPEC] * (2 * shards) + [ANY_SPEC] * shards,
        out_specs=(ANY_SPEC, ANY_SPEC, ANY_SPEC),
        scratch_shapes=[
            pltpu.VMEM((row_blocks, tile, shards * shard_rows), BF16),
            pltpu.VMEM(gate_tiles.shape, BF16),
            pltpu.VMEM(up_tiles.shape, BF16),
            pltpu.SemaphoreType.DMA((2, cols)),
            pltpu.SemaphoreType.DMA((d_hidden.shape[0] // shard_rows,)),
        ],
        compiler_params=limit(24),
        cost_estimate=pl.CostEstimate(flops=2 * shards * macs, bytes_accessed=weight_bytes, transcendentals=0),
        name="tile_grads",
    )(meta, block_rows, block_counts, *xs, *grads, *hiddens)

    mine = sum(dx.astype(F32) for dx in arrived)
    others_dx = [swap(mine.astype(BF16), "sub", s) for s in range(1, lax.axis_size("sub"))]
    features_grad = (mine + sum(dx.astype(F32) for dx in others_dx)).astype(BF16)
    return (hidden_out, gate_out, up_out, features_grad)


def solution(mesh):
    return jax.shard_map(
        on_device,
        mesh=mesh,
        in_specs=(
            P(("groups", "tok"), "blk"),
            P(("tok", "sub"), "blk", None, None, None),
            P(("tok", "sub"), "blk", None, None, None),
            P(("tok", "sub"), "blk", None),
            P(("tok", "sub"), "blk"),
            P(("groups", "blk"), ("tok", "sub")),
        ),
        out_specs=(
            P(("groups", "blk"), ("tok", "sub")),
            P(("groups", "tok", "sub"), "blk", None, None, None),
            P(("groups", "tok", "sub"), "blk", None, None, None),
            P(("groups", "tok"), "blk"),
        ),
        check_vma=False,
    )
```

profile of v0, /device:TPU:0, one launch (start us, length us, event | category | flops | bytes accessed | tf_op | source)
XLA Modules:
  0.0 84.9 jit_solution(16478812130835547552)
XLA Ops:
  0.6 3.1 %collective-permute-start = (bf16[32,2048]{1,0:T(8,128)(2,1)}, bf16[32,2048]{1,0:T(8,128)(2,1)S(1)}, u32[]{:S(2)}, u32[]{:S(2)}) collective-permute-start(bf16[32,2048]{1,0:T(8,128)(2,1)} %refs_0_.1), channel_id=1, source_target_pairs={{0,4},{4,0},{8,12},{12,8},{1,5},{5,1},{9,13},{13,9},{2,6},{6,2},{1... | collective-permute-start | bytes 393224 | tf_op jit(solution)/shard_map/ppermute | solution.py:181
  3.7 2.6 %collective-permute-start.1 = (bf16[32,2048]{1,0:T(8,128)(2,1)}, bf16[32,2048]{1,0:T(8,128)(2,1)S(1)}, u32[]{:S(2)}, u32[]{:S(2)}) collective-permute-start(bf16[32,2048]{1,0:T(8,128)(2,1)} %refs_0_.1), channel_id=1, source_target_pairs={{0,8},{4,12},{8,0},{12,4},{1,9},{5,13},{9,1},{13,5},{2,10},{6,14},... | collective-permute-start | bytes 393224 | tf_op jit(solution)/shard_map/ppermute | solution.py:181
  6.3 1.7 %collective-permute-start.4 = (bf16[64,2048]{1,0:T(8,128)(2,1)}, bf16[64,2048]{1,0:T(8,128)(2,1)S(1)}, u32[]{:S(2)}, u32[]{:S(2)}) collective-permute-start(bf16[64,2048]{1,0:T(8,128)(2,1)} %refs_2_.7), channel_id=1, source_target_pairs={{0,2},{2,0},{1,3},{3,1},{4,6},{6,4},{5,7},{7,5},{8,10},{10,8},{9,1... | collective-permute-start | bytes 786440 | tf_op jit(solution)/shard_map/ppermute | solution.py:181
  8.0 0.8 copy.26.rows_ref
  8.8 0.7 copy.27.counts_ref
  9.5 2.8 %copy-done.4 = bf16[16,1,12,128,128]{4,3,2,1,0:T(8,128)(2,1)S(1)} copy-done((bf16[16,1,12,128,128]{4,3,2,1,0:T(8,128)(2,1)S(1)}, bf16[16,1,12,128,128]{4,3,2,1,0:T(8,128)(2,1)}, u32[]{:S(2)}) %copy-start.4) | copy-done | bytes 6291480
  12.3 2.8 %copy-done.5 = bf16[16,1,12,128,128]{4,3,2,1,0:T(8,128)(2,1)S(1)} copy-done((bf16[16,1,12,128,128]{4,3,2,1,0:T(8,128)(2,1)S(1)}, bf16[16,1,12,128,128]{4,3,2,1,0:T(8,128)(2,1)}, u32[]{:S(2)}) %copy-start.5) | copy-done | bytes 6291480
  15.1 0.9 %copy-done.7 = bf16[32,2048]{1,0:T(8,128)(2,1)S(1)} copy-done((bf16[32,2048]{1,0:T(8,128)(2,1)S(1)}, bf16[32,2048]{1,0:T(8,128)(2,1)}, u32[]{:S(2)}) %copy-start.7) | copy-done | bytes 131096
  16.0 10.9 %load_forward.1 = (bf16[16,32,256]{2,1,0:T(8,128)(2,1)S(1)}, bf16[16,1,12,128,128]{4,3,2,1,0:T(8,128)(2,1)S(1)}, bf16[16,1,12,128,128]{4,3,2,1,0:T(8,128)(2,1)S(1)}) custom-call(s32[16,1,12]{2,1,0:T(1,128)S(1)} %copy.26.rows_ref, s32[16,1]{1,0:T(8,128)S(1)} %copy.27.counts_ref, bf16[32,2048]{1,0:T(8,128)(2,1)S(1)} %copy-done.7, ...), custom_call_target="tpu_custom_call" | custom-call | flops 402653184 | bytes 12582912 | tf_op jit(solution)/shard_map/load_forward/pallas_call | solution.py:198
  27.0 3.7 %forward.3.refs_0_ = bf16[16,32,256]{2,1,0:T(8,128)(2,1)S(1)} custom-call(s32[16,1,12]{2,1,0:T(1,128)S(1)} %copy.26.rows_ref, s32[16,1]{1,0:T(8,128)S(1)} %copy.27.counts_ref, bf16[32,2048]{1,0:T(8,128)(2,1)S(1)} %collective-permute-done.x_ref.refs_1_, bf16[16,1,12,128,128]{4,3,2,1,0:T(8,128)(2,1)S(1)} %get-tuple-element.22.gate_ref, ...), custom_call_target="tpu_custom_call" | custom-call | flops 402653184 | bytes 12582912 | tf_op jit(solution)/shard_map/forward/pallas_call | solution.py:215
  30.7 0.4 collective-permute-start.5
  31.0 3.7 %forward.4.refs_0_ = bf16[16,32,256]{2,1,0:T(8,128)(2,1)S(1)} custom-call(s32[16,1,12]{2,1,0:T(1,128)S(1)} %copy.26.rows_ref, s32[16,1]{1,0:T(8,128)S(1)} %copy.27.counts_ref, bf16[32,2048]{1,0:T(8,128)(2,1)S(1)} %collective-permute-done.1.x_ref.refs_2_, bf16[16,1,12,128,128]{4,3,2,1,0:T(8,128)(2,1)S(1)} %get-tuple-element.22.gate_ref, ...), custom_call_target="tpu_custom_call" | custom-call | flops 402653184 | bytes 12582912 | tf_op jit(solution)/shard_map/forward/pallas_call | solution.py:215
  34.7 0.0 copy-start.6
  34.7 1.8 %collective-permute-start.6 = (bf16[16,32,256]{2,1,0:T(8,128)(2,1)S(1)}, bf16[16,32,256]{2,1,0:T(8,128)(2,1)S(1)}, u32[]{:S(2)}, u32[]{:S(2)}) collective-permute-start(bf16[16,32,256]{2,1,0:T(8,128)(2,1)S(1)} %forward.4.refs_0_), channel_id=1, source_target_pairs={{0,2},{2,0},{1,3},{3,1},{4,6},{6,4},{5,7},{7,5},{8,10},{10,8},{9,1... | collective-permute-start | bytes 786440 | tf_op jit(solution)/shard_map/ppermute | solution.py:181
  36.5 3.7 %forward.5.refs_0_ = bf16[16,32,256]{2,1,0:T(8,128)(2,1)S(1)} custom-call(s32[16,1,12]{2,1,0:T(1,128)S(1)} %copy.26.rows_ref, s32[16,1]{1,0:T(8,128)S(1)} %copy.27.counts_ref, bf16[32,2048]{1,0:T(8,128)(2,1)S(1)} %collective-permute-done.2.x_ref.refs_3_, bf16[16,1,12,128,128]{4,3,2,1,0:T(8,128)(2,1)S(1)} %get-tuple-element.22.gate_ref, ...), custom_call_target="tpu_custom_call" | custom-call | flops 402653184 | bytes 12582912 | tf_op jit(solution)/shard_map/forward/pallas_call | solution.py:215
  40.2 0.4 collective-permute-start.7
  40.6 1.7 %collective-permute-start.3 = (bf16[16,32,256]{2,1,0:T(8,128)(2,1)S(1)}, bf16[16,32,256]{2,1,0:T(8,128)(2,1)S(1)}, u32[]{:S(2)}, u32[]{:S(2)}) collective-permute-start(bf16[16,32,256]{2,1,0:T(8,128)(2,1)S(1)} %get-tuple-element.24.refs_0_), channel_id=1, source_target_pairs={{0,2},{2,0},{1,3},{3,1},{4,6},{6,4},{5,7},{7,5},{8,10},{10,8},{9,1... | collective-permute-start | bytes 786440 | tf_op jit(solution)/shard_map/ppermute | solution.py:181
  42.3 0.1 pad_add_fusion.meta_ref
  42.4 2.8 %copy-done.1 = bf16[16,1,12,128,128]{4,3,2,1,0:T(8,128)(2,1)S(1)} copy-done((bf16[16,1,12,128,128]{4,3,2,1,0:T(8,128)(2,1)S(1)}, bf16[16,1,12,128,128]{4,3,2,1,0:T(8,128)(2,1)}, u32[]{:S(2)}) %copy-start.1) | copy-done | bytes 6291480
  45.2 2.8 %copy-done.3 = bf16[16,1,12,128,128]{4,3,2,1,0:T(8,128)(2,1)S(1)} copy-done((bf16[16,1,12,128,128]{4,3,2,1,0:T(8,128)(2,1)S(1)}, bf16[16,1,12,128,128]{4,3,2,1,0:T(8,128)(2,1)}, u32[]{:S(2)}) %copy-start.3) | copy-done | bytes 6291480
  47.9 5.7 %backward.5 = (bf16[32,2048]{1,0:T(8,128)(2,1)S(1)}, bf16[16,32,256]{2,1,0:T(8,128)(2,1)S(1)}, bf16[32,2048]{1,0:T(8,128)(2,1)S(1)}) custom-call(s32[2]{0:T(128)S(1)} %pad_add_fusion.meta_ref, s32[16,1,12]{2,1,0:T(1,128)S(1)} %copy.26.rows_ref, s32[16,1]{1,0:T(8,128)S(1)} %copy.27.counts_ref, bf16[16,1,12,128,128]{4,3,2,1,0:T(8,128)(2,1)S(1)} %copy-done.1, ...), custom_call_target="tpu_custom_call" | custom-call | flops 402653184 | bytes 12582912 | tf_op jit(solution)/shard_map/backward/pallas_call | solution.py:229
  53.6 0.7 collective-permute-start.8
  54.4 5.7 %backward.6 = (bf16[32,2048]{1,0:T(8,128)(2,1)S(1)}, bf16[16,32,256]{2,1,0:T(8,128)(2,1)S(1)}, bf16[32,2048]{1,0:T(8,128)(2,1)S(1)}) custom-call(s32[2]{0:T(128)S(1)} %pad_add_fusion.meta_ref, s32[16,1,12]{2,1,0:T(1,128)S(1)} %copy.26.rows_ref, s32[16,1]{1,0:T(8,128)S(1)} %copy.27.counts_ref, bf16[16,1,12,128,128]{4,3,2,1,0:T(8,128)(2,1)S(1)} %copy-done.1, ...), custom_call_target="tpu_custom_call" | custom-call | flops 402653184 | bytes 12582912 | tf_op jit(solution)/shard_map/backward/pallas_call | solution.py:229
  60.1 3.6 %collective-permute-start.9 = (bf16[32,2048]{1,0:T(8,128)(2,1)S(1)}, bf16[32,2048]{1,0:T(8,128)(2,1)S(1)}, u32[]{:S(2)}, u32[]{:S(2)}) collective-permute-start(bf16[32,2048]{1,0:T(8,128)(2,1)S(1)} %get-tuple-element.38), channel_id=1, source_target_pairs={{0,8},{4,12},{8,0},{12,4},{1,9},{5,13},{9,1},{13,5},{2,10},{6,14},... | collective-permute-start | bytes 393224 | tf_op jit(solution)/shard_map/ppermute | solution.py:181
  63.7 5.7 %backward.7 = (bf16[32,2048]{1,0:T(8,128)(2,1)S(1)}, bf16[16,32,256]{2,1,0:T(8,128)(2,1)S(1)}, bf16[32,2048]{1,0:T(8,128)(2,1)S(1)}) custom-call(s32[2]{0:T(128)S(1)} %pad_add_fusion.meta_ref, s32[16,1,12]{2,1,0:T(1,128)S(1)} %copy.26.rows_ref, s32[16,1]{1,0:T(8,128)S(1)} %copy.27.counts_ref, bf16[16,1,12,128,128]{4,3,2,1,0:T(8,128)(2,1)S(1)} %copy-done.1, ...), custom_call_target="tpu_custom_call" | custom-call | flops 402653184 | bytes 12582912 | tf_op jit(solution)/shard_map/backward/pallas_call | solution.py:229
  69.4 0.3 collective-permute-start.10
  69.7 5.8 %backward.4 = (bf16[32,2048]{1,0:T(8,128)(2,1)S(1)}, bf16[16,32,256]{2,1,0:T(8,128)(2,1)S(1)}, bf16[32,2048]{1,0:T(8,128)(2,1)S(1)}) custom-call(s32[2]{0:T(128)S(1)} %pad_add_fusion.meta_ref, s32[16,1,12]{2,1,0:T(1,128)S(1)} %copy.26.rows_ref, s32[16,1]{1,0:T(8,128)S(1)} %copy.27.counts_ref, bf16[16,1,12,128,128]{4,3,2,1,0:T(8,128)(2,1)S(1)} %bitcast.3, ...), custom_call_target="tpu_custom_call" | custom-call | flops 402653184 | bytes 12582912 | tf_op jit(solution)/shard_map/backward/pallas_call | solution.py:229
  75.5 0.7 collective-permute-done.10
  76.2 0.1 fusion
  76.3 0.1 collective-permute-start.11
  76.4 7.8 %tile_grads.1 = (bf16[16,1,12,128,128]{4,3,2,1,0:T(8,128)(2,1)}, bf16[16,1,12,128,128]{4,3,2,1,0:T(8,128)(2,1)}, bf16[64,2048]{1,0:T(8,128)(2,1)}) custom-call(s32[2]{0:T(128)S(1)} %pad_add_fusion.meta_ref, s32[16,1,12]{2,1,0:T(1,128)S(1)} %copy.26.rows_ref, s32[16,1]{1,0:T(8,128)S(1)} %copy.27.counts_ref, bf16[32,2048]{1,0:T(8,128)(2,1)S(1)} %copy-done.8, ...), custom_call_target="tpu_custom_call" | custom-call | flops 1610612736 | bytes 12582912 | tf_op jit(solution)/shard_map/tile_grads/pallas_call | solution.py:253
  84.2 0.7 add_convert_fusion
  (29 shorter events, 0.1 us)
Async XLA Ops:
  0.6 26.3 %collective-permute-start = (bf16[32,2048]{1,0:T(8,128)(2,1)}, bf16[32,2048]{1,0:T(8,128)(2,1)S(1)}, u32[]{:S(2)}, u32[]{:S(2)}) collective-permute-start(bf16[32,2048]{1,0:T(8,128)(2,1)} %refs_0_.1), channel_id=1, source_target_pairs={{0,4},{4,0},{8,12},{12,8},{1,5},{5,1},{9,13},{13,9},{2,6},{6,2},{1... | collective-permute-start | bytes 393224 | tf_op jit(solution)/shard_map/ppermute | solution.py:181
  3.7 27.3 %collective-permute-start.1 = (bf16[32,2048]{1,0:T(8,128)(2,1)}, bf16[32,2048]{1,0:T(8,128)(2,1)S(1)}, u32[]{:S(2)}, u32[]{:S(2)}) collective-permute-start(bf16[32,2048]{1,0:T(8,128)(2,1)} %refs_0_.1), channel_id=1, source_target_pairs={{0,8},{4,12},{8,0},{12,4},{1,9},{5,13},{9,1},{13,5},{2,10},{6,14},... | collective-permute-start | bytes 393224 | tf_op jit(solution)/shard_map/ppermute | solution.py:181
  6.3 30.2 %collective-permute-start.2 = (bf16[32,2048]{1,0:T(8,128)(2,1)}, bf16[32,2048]{1,0:T(8,128)(2,1)S(1)}, u32[]{:S(2)}, u32[]{:S(2)}) collective-permute-start(bf16[32,2048]{1,0:T(8,128)(2,1)} %refs_0_.1), channel_id=1, source_target_pairs={{0,12},{4,8},{8,4},{12,0},{1,13},{5,9},{9,5},{13,1},{2,14},{6,10},... | collective-permute-start | bytes 393224 | tf_op jit(solution)/shard_map/ppermute | solution.py:181
  6.3 36.0 %collective-permute-start.4 = (bf16[64,2048]{1,0:T(8,128)(2,1)}, bf16[64,2048]{1,0:T(8,128)(2,1)S(1)}, u32[]{:S(2)}, u32[]{:S(2)}) collective-permute-start(bf16[64,2048]{1,0:T(8,128)(2,1)} %refs_2_.7), channel_id=1, source_target_pairs={{0,2},{2,0},{1,3},{3,1},{4,6},{6,4},{5,7},{7,5},{8,10},{10,8},{9,1... | collective-permute-start | bytes 786440 | tf_op jit(solution)/shard_map/ppermute | solution.py:181
  9.5 2.8 %copy-start.4 = (bf16[16,1,12,128,128]{4,3,2,1,0:T(8,128)(2,1)S(1)}, bf16[16,1,12,128,128]{4,3,2,1,0:T(8,128)(2,1)}, u32[]{:S(2)}) copy-start(bf16[16,1,12,128,128]{4,3,2,1,0:T(8,128)(2,1)} %gate_hbm.1) | copy-start | bytes 18874372
  12.3 2.8 %copy-start.5 = (bf16[16,1,12,128,128]{4,3,2,1,0:T(8,128)(2,1)S(1)}, bf16[16,1,12,128,128]{4,3,2,1,0:T(8,128)(2,1)}, u32[]{:S(2)}) copy-start(bf16[16,1,12,128,128]{4,3,2,1,0:T(8,128)(2,1)} %up_hbm.1) | copy-start | bytes 18874372
  15.1 0.9 %copy-start.7 = (bf16[32,2048]{1,0:T(8,128)(2,1)S(1)}, bf16[32,2048]{1,0:T(8,128)(2,1)}, u32[]{:S(2)}) copy-start(bf16[32,2048]{1,0:T(8,128)(2,1)} %refs_0_.1) | copy-start | bytes 393220
  26.9 9.6 %copy-start = (bf16[16,1,12,128,128]{4,3,2,1,0:T(8,128)(2,1)}, bf16[16,1,12,128,128]{4,3,2,1,0:T(8,128)(2,1)S(1)}, u32[]{:S(2)}) copy-start(bf16[16,1,12,128,128]{4,3,2,1,0:T(8,128)(2,1)S(1)} %get-tuple-element.22.gate_ref) | copy-start | bytes 18874372
  27.0 9.6 %copy-start.2 = (bf16[16,1,12,128,128]{4,3,2,1,0:T(8,128)(2,1)}, bf16[16,1,12,128,128]{4,3,2,1,0:T(8,128)(2,1)S(1)}, u32[]{:S(2)}) copy-start(bf16[16,1,12,128,128]{4,3,2,1,0:T(8,128)(2,1)S(1)} %get-tuple-element.23.up_ref) | copy-start | bytes 18874372
  30.7 11.7 %collective-permute-start.5 = (bf16[16,32,256]{2,1,0:T(8,128)(2,1)S(1)}, bf16[16,32,256]{2,1,0:T(8,128)(2,1)S(1)}, u32[]{:S(2)}, u32[]{:S(2)}) collective-permute-start(bf16[16,32,256]{2,1,0:T(8,128)(2,1)S(1)} %forward.3.refs_0_), channel_id=1, source_target_pairs={{0,2},{2,0},{1,3},{3,1},{4,6},{6,4},{5,7},{7,5},{8,10},{10,8},{9,1... | collective-permute-start | bytes 786440 | tf_op jit(solution)/shard_map/ppermute | solution.py:181
  34.7 7.6 %copy-start.6 = (bf16[64,2048]{1,0:T(8,128)(2,1)S(1)}, bf16[64,2048]{1,0:T(8,128)(2,1)}, u32[]{:S(2)}) copy-start(bf16[64,2048]{1,0:T(8,128)(2,1)} %refs_2_.7) | copy-start | bytes 786436
  34.7 19.6 %collective-permute-start.6 = (bf16[16,32,256]{2,1,0:T(8,128)(2,1)S(1)}, bf16[16,32,256]{2,1,0:T(8,128)(2,1)S(1)}, u32[]{:S(2)}, u32[]{:S(2)}) collective-permute-start(bf16[16,32,256]{2,1,0:T(8,128)(2,1)S(1)} %forward.4.refs_0_), channel_id=1, source_target_pairs={{0,2},{2,0},{1,3},{3,1},{4,6},{6,4},{5,7},{7,5},{8,10},{10,8},{9,1... | collective-permute-start | bytes 786440 | tf_op jit(solution)/shard_map/ppermute | solution.py:181
  40.2 23.5 %collective-permute-start.7 = (bf16[16,32,256]{2,1,0:T(8,128)(2,1)S(1)}, bf16[16,32,256]{2,1,0:T(8,128)(2,1)S(1)}, u32[]{:S(2)}, u32[]{:S(2)}) collective-permute-start(bf16[16,32,256]{2,1,0:T(8,128)(2,1)S(1)} %forward.5.refs_0_), channel_id=1, source_target_pairs={{0,2},{2,0},{1,3},{3,1},{4,6},{6,4},{5,7},{7,5},{8,10},{10,8},{9,1... | collective-permute-start | bytes 786440 | tf_op jit(solution)/shard_map/ppermute | solution.py:181
  40.6 29.1 %collective-permute-start.3 = (bf16[16,32,256]{2,1,0:T(8,128)(2,1)S(1)}, bf16[16,32,256]{2,1,0:T(8,128)(2,1)S(1)}, u32[]{:S(2)}, u32[]{:S(2)}) collective-permute-start(bf16[16,32,256]{2,1,0:T(8,128)(2,1)S(1)} %get-tuple-element.24.refs_0_), channel_id=1, source_target_pairs={{0,2},{2,0},{1,3},{3,1},{4,6},{6,4},{5,7},{7,5},{8,10},{10,8},{9,1... | collective-permute-start | bytes 786440 | tf_op jit(solution)/shard_map/ppermute | solution.py:181
  42.4 2.8 %copy-start.1 = (bf16[16,1,12,128,128]{4,3,2,1,0:T(8,128)(2,1)S(1)}, bf16[16,1,12,128,128]{4,3,2,1,0:T(8,128)(2,1)}, u32[]{:S(2)}) copy-start(bf16[16,1,12,128,128]{4,3,2,1,0:T(8,128)(2,1)} %copy-done) | copy-start | bytes 18874372
  45.2 2.8 %copy-start.3 = (bf16[16,1,12,128,128]{4,3,2,1,0:T(8,128)(2,1)S(1)}, bf16[16,1,12,128,128]{4,3,2,1,0:T(8,128)(2,1)}, u32[]{:S(2)}) copy-start(bf16[16,1,12,128,128]{4,3,2,1,0:T(8,128)(2,1)} %copy-done.2) | copy-start | bytes 18874372
  53.6 21.9 %collective-permute-start.8 = (bf16[32,2048]{1,0:T(8,128)(2,1)S(1)}, bf16[32,2048]{1,0:T(8,128)(2,1)S(1)}, u32[]{:S(2)}, u32[]{:S(2)}) collective-permute-start(bf16[32,2048]{1,0:T(8,128)(2,1)S(1)} %get-tuple-element.37), channel_id=1, source_target_pairs={{0,4},{4,0},{8,12},{12,8},{1,5},{5,1},{9,13},{13,9},{2,6},{6,2},{1... | collective-permute-start | bytes 393224 | tf_op jit(solution)/shard_map/ppermute | solution.py:181
  60.1 9.6 %slice-start = ((s8[6291456]{0:T(1024)(128)(4,1)}), s8[4194304]{0:T(1024)(128)(4,1)S(1)}, s32[]{:S(2)}) async-start(s8[6291456]{0:T(1024)(128)(4,1)} %bitcast.2), calls=%async_computation | async-start | bytes 8388608
  60.1 9.6 %slice-start.1 = ((s8[6291456]{0:T(1024)(128)(4,1)}), s8[2097152]{0:T(1024)(128)(4,1)S(1)}, s32[]{:S(2)}) async-start(s8[6291456]{0:T(1024)(128)(4,1)} %bitcast.2), calls=%async_computation.1 | async-start | bytes 4194304
  60.1 15.4 %collective-permute-start.9 = (bf16[32,2048]{1,0:T(8,128)(2,1)S(1)}, bf16[32,2048]{1,0:T(8,128)(2,1)S(1)}, u32[]{:S(2)}, u32[]{:S(2)}) collective-permute-start(bf16[32,2048]{1,0:T(8,128)(2,1)S(1)} %get-tuple-element.38), channel_id=1, source_target_pairs={{0,8},{4,12},{8,0},{12,4},{1,9},{5,13},{9,1},{13,5},{2,10},{6,14},... | collective-permute-start | bytes 393224 | tf_op jit(solution)/shard_map/ppermute | solution.py:181
  69.4 7.0 %copy-start.8 = (bf16[32,2048]{1,0:T(8,128)(2,1)S(1)}, bf16[32,2048]{1,0:T(8,128)(2,1)}, u32[]{:S(2)}) copy-start(bf16[32,2048]{1,0:T(8,128)(2,1)} %refs_0_.1) | copy-start | bytes 393220
  69.4 6.8 %collective-permute-start.10 = (bf16[32,2048]{1,0:T(8,128)(2,1)S(1)}, bf16[32,2048]{1,0:T(8,128)(2,1)S(1)}, u32[]{:S(2)}, u32[]{:S(2)}) collective-permute-start(bf16[32,2048]{1,0:T(8,128)(2,1)S(1)} %get-tuple-element.39), channel_id=1, source_target_pairs={{0,12},{4,8},{8,4},{12,0},{1,13},{5,9},{9,5},{13,1},{2,14},{6,10},... | collective-permute-start | bytes 393224 | tf_op jit(solution)/shard_map/ppermute | solution.py:181
  76.3 7.9 %collective-permute-start.11 = (bf16[32,2048]{1,0:T(8,128)(2,1)S(1)}, bf16[32,2048]{1,0:T(8,128)(2,1)S(1)}, u32[]{:S(2)}, u32[]{:S(2)}) collective-permute-start(bf16[32,2048]{1,0:T(8,128)(2,1)S(1)} %fusion), channel_id=1, source_target_pairs={{0,1},{1,0},{2,3},{3,2},{4,5},{5,4},{6,7},{7,6},{8,9},{9,8},{10,11... | collective-permute-start | bytes 393224 | tf_op jit(solution)/shard_map/ppermute | solution.py:181
where the time goes:
time: 85.3 us; the launch traced here: 84.9 us
  Pallas kernels  52.6 us (62%)
  starting transfers between devices  16.3 us (19%)
  local copies, waits for them, and re-layouts  13.6 us (16%)
  other arithmetic  0.89 us (1%)
    pallas_call x4, Pallas kernels, on_device(): pl.pallas_call(functools.partial(backward_kernel, owners, s), out_shape=(...  22.9 us
    ppermute x12, starting transfers between devices, swap(): lax.ppermute(x, axis, [(i, i ^ step) for i in range(lax.axis_size(axis))])  16.3 us
    unnamed x24, local copies, waits for them, and re-layouts  13.6 us
    pallas_call x3, Pallas kernels, on_device(): pl.pallas_call(forward_kernel, out_shape=part_shape, in_specs=[SMEM_SPEC,...  11 us
    pallas_call x1, Pallas kernels, on_device(): pl.pallas_call(load_forward_kernel, out_shape=(part_shape, pltpu.VMEM(gat...  10.9 us
    pallas_call x1, Pallas kernels, on_device(): pl.pallas_call(functools.partial(tile_grads_kernel, shards), out_shape=(j...  7.82 us
  transfers between devices with their start and end apart: 12, of which 1 were waited for; matrix products, arithmetic and copies ran while one was open for 2% of the time, Pallas kernels for 62%

commit v1 on v0

v1 whole, which is shorter than its diff:
```python
import functools

import jax
import jax.numpy as jnp
from jax import lax
from jax.experimental import pallas as pl
from jax.experimental.pallas import tpu as pltpu
from jax.sharding import PartitionSpec as P

F32 = jnp.float32
BF16 = jnp.bfloat16
MIB = 1 << 20
VMEM_SPEC = pl.BlockSpec(memory_space=pltpu.VMEM)
SMEM_SPEC = pl.BlockSpec(memory_space=pltpu.SMEM)
ANY_SPEC = pl.BlockSpec(memory_space=pl.ANY)


def limit(mib):
    return pltpu.CompilerParams(vmem_limit_bytes=mib * MIB)


def lanes(index, width):
    return pl.ds(pl.multiple_of(index * width, width), width)


def chunks_of(shards):
    return [[s] for s in range(min(2, shards))] + [list(range(s, min(s + 2, shards))) for s in range(2, shards, 2)]


def for_columns(cols, body):
    def step(c, carry):
        body(c)
        return carry

    lax.fori_loop(0, cols, step, 0, unroll=cols <= 16)


def weights_of(c, gate_ref, up_ref):
    slots, rows, cols = gate_ref.shape[2:]
    return jnp.concatenate(
        [gate_ref[c, 0].reshape(slots * rows, cols), up_ref[c, 0].reshape(slots * rows, cols)], axis=1
    )


def forward_column(c, rows_ref, counts_ref, xs, gate_ref, up_ref, part_ref):
    slots, tile = gate_ref.shape[2:4]
    count = counts_ref[0, c]
    picked = []
    for k in range(slots):
        where = lanes(rows_ref[k, 0, c], tile)
        block = jnp.concatenate([x[:, where] for x in xs], axis=0)
        picked.append(jnp.where(k < count, block, jnp.zeros_like(block)))
    part_ref[c] = jnp.dot(
        jnp.concatenate(picked, axis=1), weights_of(c, gate_ref, up_ref), preferred_element_type=F32
    ).astype(BF16)


def load_forward_kernel(rows_ref, counts_ref, x_ref, gate_hbm, up_hbm, part_ref, gate_ref, up_ref, sems):
    cols = gate_ref.shape[0]

    def copies(c):
        return (
            pltpu.make_async_copy(gate_hbm.at[c], gate_ref.at[c], sems.at[0, c]),
            pltpu.make_async_copy(up_hbm.at[c], up_ref.at[c], sems.at[1, c]),
        )

    for c in range(cols):
        for copy in copies(c):
            copy.start()

    def body(c):
        for copy in copies(c):
            copy.wait()
        forward_column(c, rows_ref, counts_ref, [x_ref], gate_ref, up_ref, part_ref)

    for_columns(cols, body)


def forward_kernel(members, rows_ref, counts_ref, *refs):
    xs = refs[:members]
    gate_ref, up_ref, *_, part_ref = refs[members:]
    for_columns(
        gate_ref.shape[0], lambda c: forward_column(c, rows_ref, counts_ref, xs, gate_ref, up_ref, part_ref)
    )


def backward_kernel(owners, chunk, meta_ref, rows_ref, counts_ref, gate_ref, up_ref, *refs):
    members = len(chunk)
    parts = refs[:owners]
    cots = refs[owners : 2 * owners]
    grads_ref, hidden_ref = refs[2 * owners + 1 : 2 * owners + 3]
    dxs = refs[2 * owners + 3 : 2 * owners + 3 + members]
    cot_ref, acc_ref, sems = refs[2 * owners + 3 + members :]
    cols, _, slots, tile, _ = gate_ref.shape
    shard_rows = cot_ref.shape[0] // members
    shards_each = cots[0].shape[0] // shard_rows

    def cot_copy(m, cot, first_row):
        return pltpu.make_async_copy(
            cot.at[pl.ds(first_row, shard_rows)], cot_ref.at[pl.ds(m * shard_rows, shard_rows)], sems.at[m]
        )

    for m, step in enumerate(chunk):
        shard = meta_ref[0] ^ step
        source = (shard // shards_each) ^ meta_ref[1]
        first_row = pl.multiple_of((shard % shards_each) * shard_rows, shard_rows)
        for i, cot in enumerate(cots):

            @pl.when(source == i)
            def _(m=m, cot=cot, first_row=first_row):
                cot_copy(m, cot, first_row).start()

    acc_ref[...] = jnp.zeros_like(acc_ref)
    for m in range(members):
        cot_copy(m, cots[0], 0).wait()

    def body(c):
        total = parts[0][c].astype(F32)
        for part in parts[1:]:
            total = total + part[c].astype(F32)
        gate_value, up_value = total[:, :tile], total[:, tile:]
        cotangent = cot_ref[:, lanes(c, tile)].astype(F32)
        sig_gate = jax.nn.sigmoid(gate_value)
        act_gate = gate_value * sig_gate
        hidden_ref[:, lanes(c, tile)] = (act_gate * up_value).astype(BF16)
        gate_grad = (cotangent * up_value * sig_gate * (1.0 + gate_value * (1.0 - sig_gate))).astype(BF16)
        up_grad = (cotangent * act_gate).astype(BF16)
        grads = jnp.concatenate([gate_grad, up_grad], axis=1)
        grads_ref[c] = grads
        back = lax.dot_general(
            grads, weights_of(c, gate_ref, up_ref), (((1,), (1,)), ((), ())), preferred_element_type=F32
        )
        count = counts_ref[0, c]
        rows = [rows_ref[k, 0, c] for k in range(slots)]
        sums = []
        for k in range(slots):
            term = back[:, k * tile : (k + 1) * tile]
            sums.append(acc_ref[rows[k]] + jnp.where(k < count, term, jnp.zeros_like(term)))
        for k in range(slots):
            acc_ref[rows[k]] = sums[k]

    for_columns(cols, body)
    for r in range(acc_ref.shape[0]):
        block = acc_ref[r].astype(BF16)
        for m in range(members):
            dxs[m][:, r * tile : (r + 1) * tile] = block[m * shard_rows : (m + 1) * shard_rows]


def tile_grads_kernel(shards, chunks, meta_ref, rows_ref, counts_ref, *refs):
    xs = refs[:shards]
    grads = refs[shards : shards + len(chunks)]
    hiddens = refs[shards + len(chunks) : shards + 2 * len(chunks)]
    gate_hbm, up_hbm, hidden_hbm, turned_ref, gate_ref, up_ref, sems, hidden_sems = refs[
        shards + 2 * len(chunks) :
    ]
    cols, _, slots, tile, _ = gate_ref.shape
    shard_rows = xs[0].shape[0]
    shards_each = hidden_hbm.shape[0] // shard_rows

    def hidden_copy(i, n, m):
        return pltpu.make_async_copy(
            hiddens[n].at[pl.ds(m * shard_rows, shard_rows)],
            hidden_hbm.at[pl.ds(i * shard_rows, shard_rows)],
            hidden_sems.at[i],
        )

    for i in range(shards_each):
        step = (meta_ref[1] * shards_each + i) ^ meta_ref[0]
        for n, chunk in enumerate(chunks):
            for m, j in enumerate(chunk):

                @pl.when(step == j)
                def _(i=i, n=n, m=m):
                    hidden_copy(i, n, m).start()

    for r in range(turned_ref.shape[0]):
        block = jnp.concatenate([x[:, r * tile : (r + 1) * tile] for x in xs], axis=0)
        turned_ref[r] = block.T

    def copies(c):
        return (
            pltpu.make_async_copy(gate_ref.at[c], gate_hbm.at[c], sems.at[0, c]),
            pltpu.make_async_copy(up_ref.at[c], up_hbm.at[c], sems.at[1, c]),
        )

    def body(c):
        picked = jnp.concatenate([turned_ref[rows_ref[k, 0, c]] for k in range(slots)], axis=0)
        grad = jnp.concatenate([g[c] for g in grads], axis=0)
        found = jnp.dot(picked, grad, preferred_element_type=F32)
        count = counts_ref[0, c]
        for k in range(slots):
            term = found[k * tile : (k + 1) * tile]
            term = jnp.where(k < count, term, jnp.zeros_like(term)).astype(BF16)
            gate_ref[c, 0, k] = term[:, :tile]
            up_ref[c, 0, k] = term[:, tile:]
        for copy in copies(c):
            copy.start()

    for_columns(cols, body)
    for c in range(cols):
        for copy in copies(c):
            copy.wait()
    for i in range(shards_each):
        hidden_copy(i, 0, 0).wait()


def swap(x, axis, step):
    return lax.ppermute(x, axis, [(i, i ^ step) for i in range(lax.axis_size(axis))])


def on_device(features_in, gate_tiles, up_tiles, block_rows, block_counts, d_hidden):
    shards, owners = lax.axis_size("tok"), lax.axis_size("blk")
    chunks = chunks_of(shards)
    cols, _, slots, tile, _ = gate_tiles.shape
    shard_rows, width = features_in.shape
    row_blocks = width // tile
    meta = jnp.stack([lax.axis_index("tok"), lax.axis_index("blk")]).astype(jnp.int32)
    lists = (jnp.transpose(block_rows, (2, 1, 0)), jnp.transpose(block_counts, (1, 0)))

    xs = [features_in] + [swap(features_in, "tok", s) for s in range(1, shards)]
    cots = [d_hidden] + [swap(d_hidden, "blk", s) for s in range(1, owners)]

    macs = shard_rows * cols * slots * tile * tile * 2
    weight_bytes = 2 * cols * slots * tile * tile * 2

    def part_shape(chunk):
        return jax.ShapeDtypeStruct((cols, len(chunk) * shard_rows, 2 * tile), BF16)

    def cost(members):
        return pl.CostEstimate(flops=2 * members * macs, bytes_accessed=weight_bytes, transcendentals=0)

    part, gate_held, up_held = pl.pallas_call(
        load_forward_kernel,
        out_shape=(
            part_shape(chunks[0]),
            pltpu.VMEM(gate_tiles.shape, BF16),
            pltpu.VMEM(up_tiles.shape, BF16),
        ),
        in_specs=[SMEM_SPEC, SMEM_SPEC, VMEM_SPEC, ANY_SPEC, ANY_SPEC],
        out_specs=(VMEM_SPEC, VMEM_SPEC, VMEM_SPEC),
        scratch_shapes=[pltpu.SemaphoreType.DMA((2, cols))],
        compiler_params=limit(8),
        cost_estimate=cost(1),
        name="load_forward",
    )(
        *lists,
        features_in,
        pltpu.with_memory_space_constraint(gate_tiles, pltpu.HBM),
        pltpu.with_memory_space_constraint(up_tiles, pltpu.HBM),
    )
    def to_owners(part):
        return [swap(part, "blk", s) for s in range(1, owners)]

    parts, others = [part], [to_owners(part)]
    for n, chunk in enumerate(chunks[1:]):
        before = [cots[-1]] if n == 0 else [parts[-1], others[n - 1][-1]]
        parts.append(
            pl.pallas_call(
                functools.partial(forward_kernel, len(chunk)),
                out_shape=part_shape(chunk),
                in_specs=[SMEM_SPEC] * 2 + [VMEM_SPEC] * (len(chunk) + 2) + [ANY_SPEC] * len(before),
                out_specs=VMEM_SPEC,
                compiler_params=limit(8),
                cost_estimate=cost(len(chunk)),
                name="forward",
            )(*lists, *[xs[s] for s in chunk], gate_held, up_held, *before)
        )
        others.append(to_owners(parts[-1]))

    hiddens, grads, dxs = [], [], []
    for n, chunk in enumerate(chunks):
        rows_here = len(chunk) * shard_rows
        grad, hidden, *dx = pl.pallas_call(
            functools.partial(backward_kernel, owners, chunk),
            out_shape=(
                part_shape(chunk),
                jax.ShapeDtypeStruct((rows_here, cols * tile), BF16),
                *[jax.ShapeDtypeStruct((shard_rows, width), BF16) for _ in chunk],
            ),
            in_specs=[SMEM_SPEC] * 3 + [VMEM_SPEC] * (2 + owners) + [ANY_SPEC] * (owners + 1),
            out_specs=(VMEM_SPEC,) * (2 + len(chunk)),
            scratch_shapes=[
                pltpu.VMEM((rows_here, cols * tile), BF16),
                pltpu.VMEM((row_blocks, rows_here, tile), F32),
                pltpu.SemaphoreType.DMA((len(chunk),)),
            ],
            compiler_params=limit(8),
            cost_estimate=cost(len(chunk)),
            name="backward",
        )(meta, *lists, gate_held, up_held, parts[n], *others[n], *cots, grads[-1] if grads else part)
        hiddens.append(hidden)
        grads.append(grad)
        dxs.extend(dx)

    arrived = [dxs[0]] + [swap(dxs[s], "tok", s) for s in range(1, shards)]

    gate_out, up_out, hidden_out = pl.pallas_call(
        functools.partial(tile_grads_kernel, shards, chunks),
        out_shape=(
            jax.ShapeDtypeStruct(gate_tiles.shape, BF16),
            jax.ShapeDtypeStruct(up_tiles.shape, BF16),
            jax.ShapeDtypeStruct(d_hidden.shape, BF16),
        ),
        in_specs=[SMEM_SPEC] * 3 + [VMEM_SPEC] * (shards + len(chunks)) + [ANY_SPEC] * len(chunks),
        out_specs=(ANY_SPEC, ANY_SPEC, ANY_SPEC),
        scratch_shapes=[
            pltpu.VMEM((row_blocks, tile, shards * shard_rows), BF16),
            pltpu.VMEM(gate_tiles.shape, BF16),
            pltpu.VMEM(up_tiles.shape, BF16),
            pltpu.SemaphoreType.DMA((2, cols)),
            pltpu.SemaphoreType.DMA((d_hidden.shape[0] // shard_rows,)),
        ],
        compiler_params=limit(20),
        cost_estimate=cost(shards),
        name="tile_grads",
    )(meta, *lists, *xs, *grads, *hiddens)

    mine = sum(dx.astype(F32) for dx in arrived)
    others_dx = [swap(mine.astype(BF16), "sub", s) for s in range(1, lax.axis_size("sub"))]
    features_grad = (mine + sum(dx.astype(F32) for dx in others_dx)).astype(BF16)
    return (hidden_out, gate_out, up_out, features_grad)


def solution(mesh):
    return jax.shard_map(
        on_device,
        mesh=mesh,
        in_specs=(
            P(("groups", "tok"), "blk"),
            P(("tok", "sub"), "blk", None, None, None),
            P(("tok", "sub"), "blk", None, None, None),
            P(("tok", "sub"), "blk", None),
            P(("tok", "sub"), "blk"),
            P(("groups", "blk"), ("tok", "sub")),
        ),
        out_specs=(
            P(("groups", "blk"), ("tok", "sub")),
            P(("groups", "tok", "sub"), "blk", None, None, None),
            P(("groups", "tok", "sub"), "blk", None, None, None),
            P(("groups", "tok"), "blk"),
        ),
        check_vma=False,
    )
```

time: 85.3 us -> 79 us (0.926)
  waiting for transfers between devices: 0.7 us -> 21.2 us
  Pallas kernels: 52.6 us -> 34.4 us
  local copies, waits for them, and re-layouts: 13.6 us -> 6.95 us
  starting transfers between devices: 16.3 us -> 14.4 us
    ppermute x12 -> x11, waiting for transfers between devices: 0.7 us -> 21.2 us  [swap(): lax.ppermute(x, axis, [(i, i ^ step) for i in range(lax.axis_size(axis))])]
    pallas_call x9 -> x7, Pallas kernels: 52.6 us -> 34.4 us  [the longest x3 14.7 us: on_device(): pl.pallas_call(functools.partial(backward_kernel, owners, chunk), out_sha...]
    unnamed x24 -> x22, local copies, waits for them, and re-layouts: 13.6 us -> 6.95 us
    ppermute x12 -> x11, starting transfers between devices: 16.3 us -> 14.4 us  [swap(): lax.ppermute(x, axis, [(i, i ^ step) for i in range(lax.axis_size(axis))])]
  transfers between devices with their start and end apart: 12 -> 11, of which waited for: 1 -> 5; matrix products, arithmetic and copies ran while one was open for 2% -> 0% of each run, Pallas kernels for 62% -> 40%
where the time goes in v1:
time: 79 us; the launch traced here: 78.7 us
  Pallas kernels  34.4 us (44%)
  waiting for transfers between devices  21.2 us (27%)
  starting transfers between devices  14.4 us (18%)
  local copies, waits for them, and re-layouts  6.95 us (9%)
  other arithmetic  0.89 us (1%)
  between operations  0.79 us (1%)
    ppermute x11, waiting for transfers between devices, swap(): lax.ppermute(x, axis, [(i, i ^ step) for i in range(lax.axis_size(axis))])  21.2 us
    pallas_call x3, Pallas kernels, on_device(): pl.pallas_call(functools.partial(backward_kernel, owners, chunk), out_sha...  14.7 us
    ppermute x11, starting transfers between devices, swap(): lax.ppermute(x, axis, [(i, i ^ step) for i in range(lax.axis_size(axis))])  14.4 us
    pallas_call x1, Pallas kernels, on_device(): pl.pallas_call(load_forward_kernel, out_shape=(part_shape(chunks[0]), plt...  7.56 us
    unnamed x22, local copies, waits for them, and re-layouts  6.95 us
    pallas_call x1, Pallas kernels, on_device(): pl.pallas_call(functools.partial(tile_grads_kernel, shards, chunks), out_...  6.57 us
    pallas_call x2, Pallas kernels, on_device(): pl.pallas_call(functools.partial(forward_kernel, len(chunk)), out_shape=p...  5.61 us
  transfers between devices with their start and end apart: 11, of which 5 were waited for; matrix products, arithmetic and copies ran while one was open for 0% of the time, Pallas kernels for 40%

profile of v1, /device:TPU:0, one launch (start us, length us, event | category | flops | bytes accessed | tf_op | source)
XLA Modules:
  0.0 78.7 jit_solution(4832099664447052765)
XLA Ops:
  0.6 3.0 %collective-permute-start.4 = (bf16[64,2048]{1,0:T(8,128)(2,1)}, bf16[64,2048]{1,0:T(8,128)(2,1)S(1)}, u32[]{:S(2)}, u32[]{:S(2)}) collective-permute-start(bf16[64,2048]{1,0:T(8,128)(2,1)} %refs_2_.5), channel_id=1, source_target_pairs={{0,2},{2,0},{1,3},{3,1},{4,6},{6,4},{5,7},{7,5},{8,10},{10,8},{9,1... | collective-permute-start | bytes 786440 | tf_op jit(solution)/shard_map/ppermute | solution.py:208
  3.6 0.7 copy-done.7
  4.3 0.7 copy-done.9
  5.0 7.6 %load_forward.1 = (bf16[16,32,256]{2,1,0:T(8,128)(2,1)S(1)}, bf16[16,1,12,128,128]{4,3,2,1,0:T(8,128)(2,1)S(1)}, bf16[16,1,12,128,128]{4,3,2,1,0:T(8,128)(2,1)S(1)}) custom-call(s32[12,1,16]{2,1,0:T(1,128)S(1)} %bitcast.4, s32[1,16]{1,0:T(1,128)S(1)} %bitcast.11, bf16[32,2048]{1,0:T(8,128)(2,1)} %refs_0_.1, bf16[16,1,12,128,128]{4,3,2,1,0:T(8,128)(2,1)} %gate_hbm.1, ...), custom_call_target="tpu_custom_call" | custom-call | flops 402653184 | bytes 12582912 | tf_op jit(solution)/shard_map/load_forward/pallas_call | solution.py:232
  12.5 0.0 copy-start
  12.6 0.1 collective-permute-start.3
  12.7 2.1 %collective-permute-start = (bf16[32,2048]{1,0:T(8,128)(2,1)}, bf16[32,2048]{1,0:T(8,128)(2,1)S(1)}, u32[]{:S(2)}, u32[]{:S(2)}) collective-permute-start(bf16[32,2048]{1,0:T(8,128)(2,1)} %refs_0_.1), channel_id=1, source_target_pairs={{0,4},{4,0},{8,12},{12,8},{1,5},{5,1},{9,13},{13,9},{2,6},{6,2},{1... | collective-permute-start | bytes 393224 | tf_op jit(solution)/shard_map/ppermute | solution.py:208
  14.7 2.5 %collective-permute-start.2 = (bf16[32,2048]{1,0:T(8,128)(2,1)}, bf16[32,2048]{1,0:T(8,128)(2,1)S(1)}, u32[]{:S(2)}, u32[]{:S(2)}) collective-permute-start(bf16[32,2048]{1,0:T(8,128)(2,1)} %refs_0_.1), channel_id=1, source_target_pairs={{0,12},{4,8},{8,4},{12,0},{1,13},{5,9},{9,5},{13,1},{2,14},{6,10},... | collective-permute-start | bytes 393224 | tf_op jit(solution)/shard_map/ppermute | solution.py:208
  17.2 0.1 collective-permute-start.1
  17.3 1.2 %collective-permute-done.refs_0_.refs_1_ = bf16[32,2048]{1,0:T(8,128)(2,1)S(1)} collective-permute-done((bf16[32,2048]{1,0:T(8,128)(2,1)}, bf16[32,2048]{1,0:T(8,128)(2,1)S(1)}, u32[]{:S(2)}, u32[]{:S(2)}) %collective-permute-start) | collective-permute-done | bytes 131104 | tf_op jit(solution)/shard_map/ppermute | solution.py:208
  18.5 2.7 %forward.2.refs_0_.refs_4_ = bf16[16,32,256]{2,1,0:T(8,128)(2,1)S(1)} custom-call(s32[12,1,16]{2,1,0:T(1,128)S(1)} %bitcast.5, s32[1,16]{1,0:T(1,128)S(1)} %bitcast.12, bf16[32,2048]{1,0:T(8,128)(2,1)S(1)} %collective-permute-done.refs_0_.refs_1_, bf16[16,1,12,128,128]{4,3,2,1,0:T(8,128)(2,1)S(1)} %get-tuple-element.20.gate_ref.refs_1_.refs_2_, ...), custom_call_target="tpu_custom_call" | custom-call | flops 402653184 | bytes 12582912 | tf_op jit(solution)/shard_map/forward/pallas_call | solution.py:258
  21.3 0.0 copy-start.6
  21.3 3.0 %collective-permute-done.2.refs_1_.refs_3_ = bf16[32,2048]{1,0:T(8,128)(2,1)S(1)} collective-permute-done((bf16[32,2048]{1,0:T(8,128)(2,1)}, bf16[32,2048]{1,0:T(8,128)(2,1)S(1)}, u32[]{:S(2)}, u32[]{:S(2)}) %collective-permute-start.2) | collective-permute-done | bytes 131104 | tf_op jit(solution)/shard_map/ppermute | solution.py:208
  24.3 4.4 %collective-permute-done.1.refs_0_.refs_2_ = bf16[32,2048]{1,0:T(8,128)(2,1)S(1)} collective-permute-done((bf16[32,2048]{1,0:T(8,128)(2,1)}, bf16[32,2048]{1,0:T(8,128)(2,1)S(1)}, u32[]{:S(2)}, u32[]{:S(2)}) %collective-permute-start.1) | collective-permute-done | bytes 131104 | tf_op jit(solution)/shard_map/ppermute | solution.py:208
  28.7 2.9 %forward.3.refs_0_ = bf16[16,64,256]{2,1,0:T(8,128)(2,1)S(1)} custom-call(s32[12,1,16]{2,1,0:T(1,128)S(1)} %bitcast.6, s32[1,16]{1,0:T(1,128)S(1)} %bitcast.13, bf16[32,2048]{1,0:T(8,128)(2,1)S(1)} %collective-permute-done.1.refs_0_.refs_2_, bf16[32,2048]{1,0:T(8,128)(2,1)S(1)} %collective-permute-done.2.refs_1_.refs_3_, ...), custom_call_target="tpu_custom_call" | custom-call | flops 805306368 | bytes 12582912 | tf_op jit(solution)/shard_map/forward/pallas_call | solution.py:258
  31.6 1.6 %collective-permute-start.6 = (bf16[16,64,256]{2,1,0:T(8,128)(2,1)S(1)}, bf16[16,64,256]{2,1,0:T(8,128)(2,1)S(1)}, u32[]{:S(2)}, u32[]{:S(2)}) collective-permute-start(bf16[16,64,256]{2,1,0:T(8,128)(2,1)S(1)} %forward.3.refs_0_), channel_id=1, source_target_pairs={{0,2},{2,0},{1,3},{3,1},{4,6},{6,4},{5,7},{7,5},{8,10},{10,8},{9,1... | collective-permute-start | bytes 1572872 | tf_op jit(solution)/shard_map/ppermute | solution.py:208
  33.1 0.5 collective-permute-start.5
  33.7 0.1 pad_add_fusion.meta_ref
  33.7 2.8 %copy-done.1 = bf16[16,1,12,128,128]{4,3,2,1,0:T(8,128)(2,1)S(1)} copy-done((bf16[16,1,12,128,128]{4,3,2,1,0:T(8,128)(2,1)S(1)}, bf16[16,1,12,128,128]{4,3,2,1,0:T(8,128)(2,1)}, u32[]{:S(2)}) %copy-start.1) | copy-done | bytes 6291480
  36.5 2.8 %copy-done.4 = bf16[16,1,12,128,128]{4,3,2,1,0:T(8,128)(2,1)S(1)} copy-done((bf16[16,1,12,128,128]{4,3,2,1,0:T(8,128)(2,1)S(1)}, bf16[16,1,12,128,128]{4,3,2,1,0:T(8,128)(2,1)}, u32[]{:S(2)}) %copy-start.4) | copy-done | bytes 6291480
  39.3 4.7 %backward.3 = (bf16[16,32,256]{2,1,0:T(8,128)(2,1)S(1)}, bf16[32,2048]{1,0:T(8,128)(2,1)S(1)}, bf16[32,2048]{1,0:T(8,128)(2,1)S(1)}) custom-call(s32[2]{0:T(128)S(1)} %pad_add_fusion.meta_ref, s32[12,1,16]{2,1,0:T(1,128)S(1)} %bitcast.7, s32[1,16]{1,0:T(1,128)S(1)} %bitcast.14, bf16[16,1,12,128,128]{4,3,2,1,0:T(8,128)(2,1)S(1)} %copy-done.1, ...), custom_call_target="tpu_custom_call" | custom-call | flops 402653184 | bytes 12582912 | tf_op jit(solution)/shard_map/backward/pallas_call | solution.py:273
  44.1 5.9 %collective-permute-done.5.refs_1_ = bf16[16,32,256]{2,1,0:T(8,128)(2,1)S(1)} collective-permute-done((bf16[16,32,256]{2,1,0:T(8,128)(2,1)S(1)}, bf16[16,32,256]{2,1,0:T(8,128)(2,1)S(1)}, u32[]{:S(2)}, u32[]{:S(2)}) %collective-permute-start.5) | collective-permute-done | bytes 262176 | tf_op jit(solution)/shard_map/ppermute | solution.py:208
  49.9 4.7 %backward.4 = (bf16[16,32,256]{2,1,0:T(8,128)(2,1)S(1)}, bf16[32,2048]{1,0:T(8,128)(2,1)S(1)}, bf16[32,2048]{1,0:T(8,128)(2,1)S(1)}) custom-call(s32[2]{0:T(128)S(1)} %pad_add_fusion.meta_ref, s32[12,1,16]{2,1,0:T(1,128)S(1)} %bitcast.8, s32[1,16]{1,0:T(1,128)S(1)} %bitcast.15, bf16[16,1,12,128,128]{4,3,2,1,0:T(8,128)(2,1)S(1)} %copy-done.2, ...), custom_call_target="tpu_custom_call" | custom-call | flops 402653184 | bytes 12582912 | tf_op jit(solution)/shard_map/backward/pallas_call | solution.py:273
  54.6 0.1 collective-permute-start.7
  54.7 5.2 %backward.5 = (bf16[16,64,256]{2,1,0:T(8,128)(2,1)S(1)}, bf16[64,2048]{1,0:T(8,128)(2,1)S(1)}, bf16[32,2048]{1,0:T(8,128)(2,1)S(1)}, bf16[32,2048]{1,0:T(8,128)(2,1)S(1)}) custom-call(s32[2]{0:T(128)S(1)} %pad_add_fusion.meta_ref, s32[12,1,16]{2,1,0:T(1,128)S(1)} %bitcast.9, s32[1,16]{1,0:T(1,128)S(1)} %bitcast.16, ...), custom_call_target="tpu_custom_call" | custom-call | flops 805306368 | bytes 12582912 | tf_op jit(solution)/shard_map/backward/pallas_call | solution.py:273
  59.9 2.8 %collective-permute-start.8 = (bf16[32,2048]{1,0:T(8,128)(2,1)S(1)}, bf16[32,2048]{1,0:T(8,128)(2,1)S(1)}, u32[]{:S(2)}, u32[]{:S(2)}) collective-permute-start(bf16[32,2048]{1,0:T(8,128)(2,1)S(1)} %get-tuple-element.34), channel_id=1, source_target_pairs={{0,8},{4,12},{8,0},{12,4},{1,9},{5,13},{9,1},{13,5},{2,10},{6,14},... | collective-permute-start | bytes 393224 | tf_op jit(solution)/shard_map/ppermute | solution.py:208
  62.7 1.6 %collective-permute-start.9 = (bf16[32,2048]{1,0:T(8,128)(2,1)S(1)}, bf16[32,2048]{1,0:T(8,128)(2,1)S(1)}, u32[]{:S(2)}, u32[]{:S(2)}) collective-permute-start(bf16[32,2048]{1,0:T(8,128)(2,1)S(1)} %get-tuple-element.35), channel_id=1, source_target_pairs={{0,12},{4,8},{8,4},{12,0},{1,13},{5,9},{9,5},{13,1},{2,14},{6,10},... | collective-permute-start | bytes 393224 | tf_op jit(solution)/shard_map/ppermute | solution.py:208
  64.4 6.8 %collective-permute-done.8 = bf16[32,2048]{1,0:T(8,128)(2,1)S(1)} collective-permute-done((bf16[32,2048]{1,0:T(8,128)(2,1)S(1)}, bf16[32,2048]{1,0:T(8,128)(2,1)S(1)}, u32[]{:S(2)}, u32[]{:S(2)}) %collective-permute-start.8) | collective-permute-done | bytes 131104 | tf_op jit(solution)/shard_map/ppermute | solution.py:208
  71.2 0.1 fusion
  71.3 0.1 collective-permute-start.10
  71.3 6.6 %tile_grads.1 = (bf16[16,1,12,128,128]{4,3,2,1,0:T(8,128)(2,1)}, bf16[16,1,12,128,128]{4,3,2,1,0:T(8,128)(2,1)}, bf16[64,2048]{1,0:T(8,128)(2,1)}) custom-call(s32[2]{0:T(128)S(1)} %pad_add_fusion.meta_ref, s32[12,1,16]{2,1,0:T(1,128)S(1)} %bitcast.10, s32[1,16]{1,0:T(1,128)S(1)} %bitcast.17, bf16[32,2048]{1,0:T(8,128)(2,1)} %refs_0_.1, ...), custom_call_target="tpu_custom_call" | custom-call | flops 1610612736 | bytes 12582912 | tf_op jit(solution)/shard_map/tile_grads/pallas_call | solution.py:297
  77.9 0.7 add_convert_fusion
  (22 shorter events, 0.1 us)
Async XLA Ops:
  0.6 17.9 %collective-permute-start.4 = (bf16[64,2048]{1,0:T(8,128)(2,1)}, bf16[64,2048]{1,0:T(8,128)(2,1)S(1)}, u32[]{:S(2)}, u32[]{:S(2)}) collective-permute-start(bf16[64,2048]{1,0:T(8,128)(2,1)} %refs_2_.5), channel_id=1, source_target_pairs={{0,2},{2,0},{1,3},{3,1},{4,6},{6,4},{5,7},{7,5},{8,10},{10,8},{9,1... | collective-permute-start | bytes 786440 | tf_op jit(solution)/shard_map/ppermute | solution.py:208
  3.6 0.7 copy-start.7
  4.3 0.7 copy-start.9
  12.5 16.1 %copy-start = (bf16[16,1,12,128,128]{4,3,2,1,0:T(8,128)(2,1)}, bf16[16,1,12,128,128]{4,3,2,1,0:T(8,128)(2,1)S(1)}, u32[]{:S(2)}) copy-start(bf16[16,1,12,128,128]{4,3,2,1,0:T(8,128)(2,1)S(1)} %get-tuple-element.20.gate_ref.refs_1_.refs_2_) | copy-start | bytes 18874372
  12.6 16.1 %copy-start.3 = (bf16[16,1,12,128,128]{4,3,2,1,0:T(8,128)(2,1)}, bf16[16,1,12,128,128]{4,3,2,1,0:T(8,128)(2,1)S(1)}, u32[]{:S(2)}) copy-start(bf16[16,1,12,128,128]{4,3,2,1,0:T(8,128)(2,1)S(1)} %get-tuple-element.21.up_ref.refs_2_.refs_3_) | copy-start | bytes 18874372
  12.6 16.1 %collective-permute-start.3 = (bf16[16,32,256]{2,1,0:T(8,128)(2,1)S(1)}, bf16[16,32,256]{2,1,0:T(8,128)(2,1)S(1)}, u32[]{:S(2)}, u32[]{:S(2)}) collective-permute-start(bf16[16,32,256]{2,1,0:T(8,128)(2,1)S(1)} %get-tuple-element.22.refs_0_.refs_4_), channel_id=1, source_target_pairs={{0,2},{2,0},{1,3},{3,1},{4,6},{6,4},{5,7},{7,5},{8,10},{10,8},{9,1... | collective-permute-start | bytes 786440 | tf_op jit(solution)/shard_map/ppermute | solution.py:208
  12.7 5.9 %collective-permute-start = (bf16[32,2048]{1,0:T(8,128)(2,1)}, bf16[32,2048]{1,0:T(8,128)(2,1)S(1)}, u32[]{:S(2)}, u32[]{:S(2)}) collective-permute-start(bf16[32,2048]{1,0:T(8,128)(2,1)} %refs_0_.1), channel_id=1, source_target_pairs={{0,4},{4,0},{8,12},{12,8},{1,5},{5,1},{9,13},{13,9},{2,6},{6,2},{1... | collective-permute-start | bytes 393224 | tf_op jit(solution)/shard_map/ppermute | solution.py:208
  14.7 9.5 %collective-permute-start.2 = (bf16[32,2048]{1,0:T(8,128)(2,1)}, bf16[32,2048]{1,0:T(8,128)(2,1)S(1)}, u32[]{:S(2)}, u32[]{:S(2)}) collective-permute-start(bf16[32,2048]{1,0:T(8,128)(2,1)} %refs_0_.1), channel_id=1, source_target_pairs={{0,12},{4,8},{8,4},{12,0},{1,13},{5,9},{9,5},{13,1},{2,14},{6,10},... | collective-permute-start | bytes 393224 | tf_op jit(solution)/shard_map/ppermute | solution.py:208
  17.2 11.5 %collective-permute-start.1 = (bf16[32,2048]{1,0:T(8,128)(2,1)}, bf16[32,2048]{1,0:T(8,128)(2,1)S(1)}, u32[]{:S(2)}, u32[]{:S(2)}) collective-permute-start(bf16[32,2048]{1,0:T(8,128)(2,1)} %refs_0_.1), channel_id=1, source_target_pairs={{0,8},{4,12},{8,0},{12,4},{1,9},{5,13},{9,1},{13,5},{2,10},{6,14},... | collective-permute-start | bytes 393224 | tf_op jit(solution)/shard_map/ppermute | solution.py:208
  21.3 12.5 %copy-start.6 = (bf16[64,2048]{1,0:T(8,128)(2,1)S(1)}, bf16[64,2048]{1,0:T(8,128)(2,1)}, u32[]{:S(2)}) copy-start(bf16[64,2048]{1,0:T(8,128)(2,1)} %refs_2_.5) | copy-start | bytes 786436
  21.3 12.5 %copy-start.8 = (s32[16,1,12]{0,1,2:T(1,128)S(1)}, s32[16,1,12]{0,1,2:T(1,128)}, u32[]{:S(2)}) copy-start(s32[16,1,12]{0,1,2:T(1,128)} %param.9) | copy-start | bytes 2308
  21.3 12.4 %copy-start.10 = (s32[16,1]{0,1:T(1,128)S(1)}, s32[16,1]{0,1:T(1,128)}, u32[]{:S(2)}) copy-start(s32[16,1]{0,1:T(1,128)} %param.10) | copy-start | bytes 196
  31.6 23.2 %collective-permute-start.6 = (bf16[16,64,256]{2,1,0:T(8,128)(2,1)S(1)}, bf16[16,64,256]{2,1,0:T(8,128)(2,1)S(1)}, u32[]{:S(2)}, u32[]{:S(2)}) collective-permute-start(bf16[16,64,256]{2,1,0:T(8,128)(2,1)S(1)} %forward.3.refs_0_), channel_id=1, source_target_pairs={{0,2},{2,0},{1,3},{3,1},{4,6},{6,4},{5,7},{7,5},{8,10},{10,8},{9,1... | collective-permute-start | bytes 1572872 | tf_op jit(solution)/shard_map/ppermute | solution.py:208
  33.1 16.8 %collective-permute-start.5 = (bf16[16,32,256]{2,1,0:T(8,128)(2,1)S(1)}, bf16[16,32,256]{2,1,0:T(8,128)(2,1)S(1)}, u32[]{:S(2)}, u32[]{:S(2)}) collective-permute-start(bf16[16,32,256]{2,1,0:T(8,128)(2,1)S(1)} %forward.2.refs_0_.refs_4_), channel_id=1, source_target_pairs={{0,2},{2,0},{1,3},{3,1},{4,6},{6,4},{5,7},{7,5},{8,10},{10,8},{9,1... | collective-permute-start | bytes 786440 | tf_op jit(solution)/shard_map/ppermute | solution.py:208
  33.7 2.8 %copy-start.1 = (bf16[16,1,12,128,128]{4,3,2,1,0:T(8,128)(2,1)S(1)}, bf16[16,1,12,128,128]{4,3,2,1,0:T(8,128)(2,1)}, u32[]{:S(2)}) copy-start(bf16[16,1,12,128,128]{4,3,2,1,0:T(8,128)(2,1)} %copy-done) | copy-start | bytes 18874372
  36.5 2.8 %copy-start.4 = (bf16[16,1,12,128,128]{4,3,2,1,0:T(8,128)(2,1)S(1)}, bf16[16,1,12,128,128]{4,3,2,1,0:T(8,128)(2,1)}, u32[]{:S(2)}) copy-start(bf16[16,1,12,128,128]{4,3,2,1,0:T(8,128)(2,1)} %copy-done.3) | copy-start | bytes 18874372
  39.3 10.6 %copy-start.2 = (bf16[16,1,12,128,128]{4,3,2,1,0:T(8,128)(2,1)S(1)}, bf16[16,1,12,128,128]{4,3,2,1,0:T(8,128)(2,1)}, u32[]{:S(2)}) copy-start(bf16[16,1,12,128,128]{4,3,2,1,0:T(8,128)(2,1)} %copy-done) | copy-start | bytes 18874372
  39.3 10.6 %copy-start.5 = (bf16[16,1,12,128,128]{4,3,2,1,0:T(8,128)(2,1)S(1)}, bf16[16,1,12,128,128]{4,3,2,1,0:T(8,128)(2,1)}, u32[]{:S(2)}) copy-start(bf16[16,1,12,128,128]{4,3,2,1,0:T(8,128)(2,1)} %copy-done.3) | copy-start | bytes 18874372
  54.6 9.7 %collective-permute-start.7 = (bf16[32,2048]{1,0:T(8,128)(2,1)S(1)}, bf16[32,2048]{1,0:T(8,128)(2,1)S(1)}, u32[]{:S(2)}, u32[]{:S(2)}) collective-permute-start(bf16[32,2048]{1,0:T(8,128)(2,1)S(1)} %get-tuple-element.33), channel_id=1, source_target_pairs={{0,4},{4,0},{8,12},{12,8},{1,5},{5,1},{9,13},{13,9},{2,6},{6,2},{1... | collective-permute-start | bytes 393224 | tf_op jit(solution)/shard_map/ppermute | solution.py:208
  59.9 11.2 %collective-permute-start.8 = (bf16[32,2048]{1,0:T(8,128)(2,1)S(1)}, bf16[32,2048]{1,0:T(8,128)(2,1)S(1)}, u32[]{:S(2)}, u32[]{:S(2)}) collective-permute-start(bf16[32,2048]{1,0:T(8,128)(2,1)S(1)} %get-tuple-element.34), channel_id=1, source_target_pairs={{0,8},{4,12},{8,0},{12,4},{1,9},{5,13},{9,1},{13,5},{2,10},{6,14},... | collective-permute-start | bytes 393224 | tf_op jit(solution)/shard_map/ppermute | solution.py:208
  62.7 8.4 %collective-permute-start.9 = (bf16[32,2048]{1,0:T(8,128)(2,1)S(1)}, bf16[32,2048]{1,0:T(8,128)(2,1)S(1)}, u32[]{:S(2)}, u32[]{:S(2)}) collective-permute-start(bf16[32,2048]{1,0:T(8,128)(2,1)S(1)} %get-tuple-element.35), channel_id=1, source_target_pairs={{0,12},{4,8},{8,4},{12,0},{1,13},{5,9},{9,5},{13,1},{2,14},{6,10},... | collective-permute-start | bytes 393224 | tf_op jit(solution)/shard_map/ppermute | solution.py:208
  71.3 6.7 %collective-permute-start.10 = (bf16[32,2048]{1,0:T(8,128)(2,1)S(1)}, bf16[32,2048]{1,0:T(8,128)(2,1)S(1)}, u32[]{:S(2)}, u32[]{:S(2)}) collective-permute-start(bf16[32,2048]{1,0:T(8,128)(2,1)S(1)} %fusion), channel_id=1, source_target_pairs={{0,1},{1,0},{2,3},{3,2},{4,5},{5,4},{6,7},{7,6},{8,9},{9,8},{10,11... | collective-permute-start | bytes 393224 | tf_op jit(solution)/shard_map/ppermute | solution.py:208
